TPU v7x, 256 devices: a whole 4x4x8 slice. The times are simulated.
256 devices in a mesh: seq: 16 (over x, y), nbr: 16 (over z, core).
Axes of the slice: x: 4, y: 4, z: 8, core: 2. Of those that a mesh axis runs over, the one named last changes fastest.
Arguments:
- tokens: bfloat16 [8192, 4096], P(('seq', 'nbr')), may hold values from -7 to 7
- nbr_embed: bfloat16 [256, 128, 896], P('seq', 'nbr'), may hold values from -7 to 7
- neighbour_table: int32 [128, 2], P('seq'), may hold values from 0 to 255, as said below
- valid_counts: int32 [128], replicated, may hold values from 1 to 2
- dec_proj: bfloat16 [4096, 3, 4096], P(None, None, 'nbr'), may hold values from -1 to 1
- enc_query: bfloat16 [896, 4096], P(None, 'nbr'), may hold values from -2 to 2
- enc_out: bfloat16 [4096, 896], P('nbr'), may hold values from -0.09375 to 0.09375
- enc_gain: float32 [896], replicated, may hold values from 0.1 to 1.9
- nbr_proj: bfloat16 [896, 2, 4096], P(None, None, 'nbr'), may hold values from -2 to 2
- out_proj: bfloat16 [4096, 4096], P('nbr'), may hold values from -0.09375 to 0.09375
Outputs:
- cross_out: bfloat16 [8192, 4096], P(('seq', 'nbr'))
- encoded: bfloat16 [32768, 896], P(('seq', 'nbr'))
Inputs may be any that keep to these rules, and one draw needn't show every extreme that they name: `neighbour_table`: for each block b of 8 groups in order, the entries of those groups are a permutation of the neighbour rows b * 16 to (b + 1) * 16 - 1.
All inputs are finite; a program needn't handle non-finite values.
Results may differ from a plain program's by a relative error of at most 0.025.
Values may be sent and summed in bfloat16 or wider, within the bound.
A program may use at most 128 MiB of HBM per device.

v0:
```python
import jax
import jax.numpy as jnp
from jax import lax
from jax.sharding import PartitionSpec as P

HEAD_DIM = 128
GROUP = 64
NLEN = 128
SEQ_LEN = 2048


def passed_along(block, axis, distance):
    devices = range(lax.axis_size(axis))
    route = [(i - distance, i) for i in devices if i - distance in devices]
    return lax.ppermute(block, axis, route)


def plain_softmax(scores):
    peak = jnp.max(scores, axis=-1, keepdims=True)
    raised = jnp.exp(scores - peak)
    return (raised / jnp.sum(raised, axis=-1, keepdims=True)).astype(jnp.bfloat16)


def masked_softmax(scores, allowed):
    live = jnp.any(allowed, axis=-1, keepdims=True)
    peak = jnp.max(jnp.where(allowed, scores, -1e30), axis=-1, keepdims=True)
    peak = jnp.where(live, peak, 0.0)
    raised = jnp.where(allowed, jnp.exp(scores - peak), 0.0)
    denominator = jnp.where(live, jnp.sum(raised, axis=-1, keepdims=True), 1.0)
    return (raised / denominator).astype(jnp.bfloat16)


def normed_rows(raw_rows, partial_sum, enc_gain):
    combined = raw_rows.astype(jnp.float32) + partial_sum
    factor = lax.rsqrt(jnp.mean(combined * combined, axis=-1, keepdims=True) + 1e-06)
    return (combined * factor * enc_gain).astype(jnp.bfloat16)


def local(
    tokens,
    nbr_embed,
    neighbour_table,
    valid_counts,
    dec_proj,
    enc_query,
    enc_out,
    enc_gain,
    nbr_proj,
    out_proj,
):
    n_nbr = lax.axis_size("nbr")
    seq_index = lax.axis_index("seq")
    member = lax.axis_index("nbr")
    model_width = tokens.shape[1]
    local_width = dec_proj.shape[2]
    head_dev = local_width // HEAD_DIM
    scale = 1.0 / HEAD_DIM**0.5
    dec_flat = dec_proj.reshape(model_width, 3 * local_width)
    projected = jnp.dot(
        lax.all_gather(tokens, "nbr", axis=0, tiled=True),
        dec_flat,
        preferred_element_type=jnp.float32,
    ).astype(jnp.bfloat16)
    tok_grp = projected.shape[0]
    ch_grp = tok_grp // GROUP
    queries = projected[:, :local_width]
    cond_key = projected[:, local_width : 2 * local_width].reshape(
        ch_grp, GROUP, head_dev, HEAD_DIM
    )
    cond_value = projected[:, 2 * local_width :].reshape(ch_grp, GROUP, head_dev, HEAD_DIM)
    grp_embed = lax.all_gather(nbr_embed, "nbr", axis=1, tiled=True)
    nb_grp = grp_embed.shape[0]
    enc_width = grp_embed.shape[2]
    row_ids = neighbour_table.reshape(-1) - seq_index * nb_grp
    ordered = jnp.take(grp_embed, row_ids, axis=0).reshape(-1, enc_width)
    enc_queries = jnp.dot(ordered, enc_query, preferred_element_type=jnp.float32).astype(
        jnp.bfloat16
    )
    enc_queries = enc_queries.reshape(ch_grp, -1, head_dev, HEAD_DIM)
    enc_scores = (
        jnp.einsum("cqhd,ckhd->chqk", enc_queries, cond_key, preferred_element_type=jnp.float32)
        * scale
    )
    enc_weights = plain_softmax(enc_scores)
    enc_att = jnp.einsum(
        "chqk,ckhd->cqhd", enc_weights, cond_value, preferred_element_type=jnp.float32
    ).astype(jnp.bfloat16)
    enc_att = enc_att.reshape(-1, local_width)
    share_rows = enc_att.shape[0] // n_nbr
    summed = lax.psum(jnp.dot(enc_att, enc_out, preferred_element_type=jnp.float32), "nbr")
    encoded_all = normed_rows(ordered, summed, enc_gain)
    encoded_mine = lax.dynamic_slice_in_dim(encoded_all, member * share_rows, share_rows, 0)
    nbr_kv = jnp.dot(
        encoded_all,
        nbr_proj.reshape(enc_width, 2 * local_width),
        preferred_element_type=jnp.float32,
    ).astype(jnp.bfloat16)
    nbr_kv = nbr_kv.reshape(ch_grp, -1, 2 * local_width)
    previous = passed_along(nbr_kv[-1], "seq", 1)
    kv_ext = jnp.concatenate([previous[None], nbr_kv], axis=0)
    key_rows = kv_ext.shape[1]
    kv_ext = kv_ext.reshape(ch_grp + 1, key_rows, 2, head_dev, HEAD_DIM)
    counts_pad = jnp.concatenate([jnp.zeros((1,), jnp.int32), valid_counts], axis=0)
    counts_ext = lax.dynamic_slice_in_dim(counts_pad, seq_index * ch_grp, ch_grp + 1, 0)
    query_pad = jnp.concatenate(
        [
            jnp.zeros((1, local_width), jnp.bfloat16),
            queries,
            jnp.zeros((GROUP - 1, local_width), jnp.bfloat16),
        ],
        axis=0,
    )
    query_pad = query_pad.reshape(ch_grp + 1, GROUP, head_dev, HEAD_DIM)
    local_ids = jnp.arange((ch_grp + 1) * GROUP, dtype=jnp.int32) - 1
    global_ids = seq_index * tok_grp + local_ids
    active = (local_ids >= 0) & (local_ids < tok_grp) & (global_ids % SEQ_LEN >= GROUP - 1)
    active = active.reshape(ch_grp + 1, GROUP)
    key_slot = jnp.arange(key_rows, dtype=jnp.int32) // NLEN
    slot_live = key_slot[None, :] < counts_ext[:, None]
    allowed = active[:, None, :, None] & slot_live[:, None, None, :]
    cca_scores = (
        jnp.einsum(
            "bqhd,bkhd->bhqk", query_pad, kv_ext[:, :, 0], preferred_element_type=jnp.float32
        )
        * scale
    )
    cca_weights = masked_softmax(cca_scores, allowed)
    cca_att = jnp.einsum(
        "bhqk,bkhd->bqhd", cca_weights, kv_ext[:, :, 1], preferred_element_type=jnp.float32
    ).astype(jnp.bfloat16)
    cca_att = cca_att.reshape(-1, local_width)[1 : tok_grp + 1]
    cross_out = lax.psum_scatter(
        jnp.dot(cca_att, out_proj, preferred_element_type=jnp.float32).astype(jnp.bfloat16),
        "nbr",
        scatter_dimension=0,
        tiled=True,
    )
    return (cross_out, encoded_mine)


def solution(mesh):
    return jax.shard_map(
        local,
        mesh=mesh,
        in_specs=(
            P(("seq", "nbr"), None),
            P("seq", "nbr", None),
            P("seq", None),
            P(),
            P(None, None, "nbr"),
            P(None, "nbr"),
            P("nbr", None),
            P(),
            P(None, None, "nbr"),
            P("nbr", None),
        ),
        out_specs=(P(("seq", "nbr"), None), P(("seq", "nbr"), None)),
        check_vma=False,
    )
```

profile of v0, /device:TPU:6, one launch (start us, length us, event | category | flops | bytes accessed | tf_op | source)
XLA Modules:
  0.0 344.8 jit_solution(4652820570967814219)
XLA Ops:
  7.2 0.7 all-gather.3.cloned.1.call-update
  8.0 0.7 all-gather.5.cloned.1.call-update
  8.7 0.7 broadcast_subtract_fusion
  9.6 8.8 %copy.33 = bf16[4096,3,256]{0,2,1:T(8,128)(2,1)} copy(bf16[4096,3,256]{2,0,1:T(8,128)(2,1)} %param.14) | data formatting | bytes 12582912 | tf_op args[4]
  18.5 35.8 %all-gather.3.cloned.1.call-done = bf16[16,128,896]{2,1,0:T(8,128)(2,1)} async-done(((bf16[16,8,896]{2,1,0:T(8,128)(2,1)}), bf16[16,128,896]{2,1,0:T(8,128)(2,1)}) %all-gather.3.cloned.1.call-update) | async-done | bytes 3670032 | tf_op jit(solution)/shard_map/all_gather | solution.py:71
  54.3 4.8 %gather_fusion = bf16[16,128,896]{2,1,0:T(8,128)(2,1)} fusion(bf16[16,128,896]{2,1,0:T(8,128)(2,1)} %all-gather.3.cloned.1.call-done, s32[1024]{0:T(1024)S(1)} %pad_clamp_fusion), kind=kCustom, calls=%fused_computation | custom fusion | bytes 7340096 | tf_op jit(solution)/shard_map/jit(_take)/gather | solution.py:75
  59.1 2.4 bitcast_select_fusion
  61.6 2.3 convolution_convert_fusion.2
  63.8 1.3 reshape.164
  65.2 31.5 %all-gather.5.cloned.1.call-done = bf16[512,4096]{1,0:T(8,128)(2,1)} async-done(((bf16[32,4096]{1,0:T(8,128)(2,1)}), bf16[512,4096]{1,0:T(8,128)(2,1)}) %all-gather.5.cloned.1.call-update) | async-done | bytes 4194320 | tf_op jit(solution)/shard_map/all_gather | solution.py:60
  96.7 7.5 %convolution_convert_fusion.4 = bf16[512,768]{1,0:T(8,128)(2,1)S(1)} fusion(bf16[512,4096]{1,0:T(8,128)(2,1)} %all-gather.5.cloned.1.call-done, bf16[4096,768]{0,1:T(8,128)(2,1)} %bitcast.49), kind=kOutput, calls=%fused_computation.13 | convolution fusion | flops 3221618688 | bytes 11272192 | tf_op jit(solution)/shard_map/dot_general | solution.py:59
  104.2 0.9 fusion.25
  105.1 1.0 reshape.165
  106.6 1.0 copy-done.5
  107.9 1.0 reshape.163
  108.9 2.0 fusion.2
  112.0 4.3 %fusion.27 = f32[2048,896]{1,0:T(8,128)} fusion(bf16[2048,256]{0,1:T(8,128)(2,1)S(1)} %bitcast.50, bf16[256,896]{1,0:T(8,128)(2,1)S(1)} %copy-done.9), kind=kOutput, calls=%fused_computation.72 | convolution fusion | flops 939524096 | bytes 8847360 | tf_op jit(solution)/shard_map/dot_general | solution.py:90
  116.5 0.9 copy-done.7
  117.4 1.1 copy.43
  119.0 127.7 %all-reduce.2.cloned.1.call-done = f32[2048,896]{1,0:T(8,128)} async-done(((f32[2048,896]{1,0:T(8,128)}), f32[2048,896]{1,0:T(8,128)}) %all-reduce.2.cloned.1.call-update) | async-done | bytes 7340048 | tf_op jit(solution)/shard_map/psum | solution.py:90
  246.6 5.5 %multiply_reduce_fusion = f32[2048]{0:T(1024)S(1)} fusion(f32[2048,896]{1,0:T(8,128)} %all-reduce.2.cloned.1.call-done, bf16[16,128,896]{2,1,0:T(8,128)(2,1)} %gather_fusion, pred[2048]{0:T(1024)(128)(4,1)S(1)} %broadcast_bitcast_fusion), kind=kLoop, calls=%fused_computation.3 | loop fusion | flops 9172992 | bytes 11020288 | tf_op jit(solution)/shard_map/reduce_sum | solution.py:35
  252.2 1.9 copy-done.2
  254.1 1.9 multiply_convert_fusion
  256.0 2.4 convolution_convert_fusion.1
  258.4 1.3 copy-done.4
  259.7 3.4 collective-permute-start
  263.9 4.0 %concatenate.15 = bf16[8,256,2,2,128]{4,3,2,1,0:T(2,128)(2,1)} reshape(bf16[2048,512]{1,0:T(8,128)(2,1)} %copy-done.4) | data formatting | bytes 4194304 | tf_op jit(solution)/shard_map/concatenate | solution.py:100
  267.9 2.6 collective-permute-done
  270.6 2.3 copy_dynamic-update-slice_fusion
  275.0 3.2 convolution_convert_fusion
  278.2 1.6 constant_dynamic-slice_fusion
  279.8 58.4 %reduce-scatter.2.cloned.1.call-done = bf16[32,4096]{1,0:T(8,128)(2,1)} async-done(((bf16[512,4096]{1,0:T(8,128)(2,1)}), bf16[32,4096]{1,0:T(8,128)(2,1)}) %reduce-scatter.2.cloned.1.call-update) | async-done | bytes 262160 | tf_op jit(solution)/shard_map/reduce_scatter | solution.py:132
  (62 shorter events, 5.8 us)
Async XLA Ops:
  7.2 267.8 %copy-start = (bf16[256,4096]{1,0:T(8,128)(2,1)S(1)}, bf16[256,4096]{1,0:T(8,128)(2,1)}, u32[]{:S(2)}) copy-start(bf16[256,4096]{1,0:T(8,128)(2,1)} %param.19) | copy-start | bytes 6291460
  7.2 47.1 %all-gather.3.cloned.1.call-start = ((), (), s32[]{:S(2)}) async-start(), calls=%async_computation.1 | async-start | bytes 3899392 | tf_op jit(solution)/shard_map/all_gather | solution.py:71
  7.9 88.8 %all-gather.5.cloned.1.call-start = ((), (), s32[]{:S(2)}) async-start(), calls=%async_computation.2 | async-start | bytes 4456448 | tf_op jit(solution)/shard_map/all_gather | solution.py:60
  8.7 238.0 %all-reduce.2.cloned.1.call-start = ((), (), s32[]{:S(2)}) async-start(), calls=%async_computation.3 | async-start | bytes 14680064 | tf_op jit(solution)/shard_map/psum | solution.py:90
  59.1 2.4 copy-start.12
  106.6 1.0 copy-start.5
  110.9 1.0 copy-start.9
  116.3 1.2 copy-start.7
  116.3 2.3 copy-start.11
  116.3 221.9 %reduce-scatter.2.cloned.1.call-start = ((), (), s32[]{:S(2)}) async-start(), calls=%async_computation.4 | async-start | bytes 4456448 | tf_op jit(solution)/shard_map/reduce_scatter | solution.py:132
  119.0 133.2 %copy-start.10 = (f32[896]{0:T(1024)S(1)}, f32[896]{0:T(1024)}, u32[]{:S(2)}) copy-start(f32[896]{0:T(1024)} %param.17) | copy-start | bytes 10756
  246.6 5.5 %copy-start.1 = (bf16[16,128,896]{2,1,0:T(8,128)(2,1)S(1)}, bf16[16,128,896]{2,1,0:T(8,128)(2,1)}, u32[]{:S(2)}) copy-start(bf16[16,128,896]{2,1,0:T(8,128)(2,1)} %gather_fusion) | copy-start | bytes 11010052
  246.6 7.4 %copy-start.2 = (f32[2048,896]{1,0:T(8,128)S(1)}, f32[2048,896]{1,0:T(8,128)}, u32[]{:S(2)}) copy-start(f32[2048,896]{1,0:T(8,128)} %all-reduce.2.cloned.1.call-done) | copy-start | bytes 22020100
  254.1 1.9 copy-start.8
  256.0 2.4 copy-start.3
  256.0 7.6 %copy-start.6 = (bf16[512,256]{1,0:T(8,128)(2,1)S(1)}, bf16[512,256]{1,0:T(8,128)(2,1)}, u32[]{:S(2)}) copy-start(bf16[512,256]{1,0:T(8,128)(2,1)} %get-tuple-element.2) | copy-start | bytes 786436
  258.4 1.3 copy-start.4
  259.7 10.8 %collective-permute-start = (bf16[256,512]{1,0:T(8,128)(2,1)S(1)}, bf16[256,512]{1,0:T(8,128)(2,1)S(1)}, u32[]{:S(2)}, u32[]{:S(2)}) collective-permute-start(bf16[256,512]{1,0:T(8,128)(2,1)S(1)} %slice.34), channel_id=1, source_target_pairs={{0,16},{16,32},{32,48},{48,64},{64,80},{80,96},{96,112},{112,128},... | collective-permute-start | bytes 786440 | tf_op jit(solution)/shard_map/ppermute | solution.py:15
Sparse Core Ops, SparseCore 0:
  9.8 44.4 all-gather.2
  56.1 40.5 all-gather.4
  116.4 130.1 all-reduce.1
  278.3 59.8 reduce-scatter.1
where the time goes:
time: 345 us
  waiting for transfers between devices  257 us (74%)
  local copies, waits for them, and re-layouts  34 us (10%)
  matrix products  23.3 us (7%)
  between operations  14.1 us (4%)
  other arithmetic  12.2 us (4%)
  starting transfers between devices  3.72 us (1%)
    psum x1, waiting for transfers between devices, local(): lax.psum(jnp.dot(enc_att, enc_out, preferred_element_type=jnp.float32), '...  128 us
    reduce_scatter x1, waiting for transfers between devices, local(): lax.psum_scatter(jnp.dot(cca_att, out_proj, preferred_element_type=jnp.fl...  58.4 us
    all_gather x1, waiting for transfers between devices, local(): grp_embed = lax.all_gather(nbr_embed, 'nbr', axis=1, tiled=True)  35.8 us
    all_gather x1, waiting for transfers between devices, local(): lax.all_gather(tokens, 'nbr', axis=0, tiled=True)  31.5 us
    unnamed x31, local copies, waits for them, and re-layouts  15.5 us
    dot_general x1, matrix products, local(): jnp.dot(lax.all_gather(tokens, 'nbr', axis=0, tiled=True), dec_flat, pref...  7.51 us
  transfers between devices with their start and end apart: 5, of which 5 were waited for; matrix products, arithmetic and copies ran while one was open for 8% of the time, Pallas kernels for 0%

commit v1 on v0

--- a/solution.py
+++ b/solution.py
@@ -68,7 +68,9 @@
         ch_grp, GROUP, head_dev, HEAD_DIM
     )
     cond_value = projected[:, 2 * local_width :].reshape(ch_grp, GROUP, head_dev, HEAD_DIM)
-    grp_embed = lax.all_gather(nbr_embed, "nbr", axis=1, tiled=True)
+    grp_embed = jnp.concatenate(
+        lax.all_to_all(jnp.stack([nbr_embed] * lax.axis_size("nbr")), "nbr", 0, 0), axis=1
+    )
     nb_grp = grp_embed.shape[0]
     enc_width = grp_embed.shape[2]
     row_ids = neighbour_table.reshape(-1) - seq_index * nb_grp

time: 345 us -> 386 us (1.12)
  waiting for transfers between devices: 257 us -> 283 us
  starting transfers between devices: 3.72 us -> 12.4 us
  local copies, waits for them, and re-layouts: 34 us -> 41.6 us
    all_to_all x0 -> x1, waiting for transfers between devices: none -> 92.9 us  [local(): lax.all_to_all(jnp.stack([nbr_embed] * lax.axis_size('nbr')), 'nbr', 0, 0)]
    all_gather x1 -> x0, waiting for transfers between devices: 35.8 us -> none  [local(): grp_embed = lax.all_gather(nbr_embed, 'nbr', axis=1, tiled=True)]
    all_gather x1, waiting for transfers between devices: 31.5 us -> 0.02 us  [local(): lax.all_gather(tokens, 'nbr', axis=0, tiled=True)]
    all_to_all x0 -> x1, starting transfers between devices: none -> 8.75 us  [local(): lax.all_to_all(jnp.stack([nbr_embed] * lax.axis_size('nbr')), 'nbr', 0, 0)]
    all_to_all x0 -> x1, local copies, waits for them, and re-layouts: none -> 4.36 us  [local(): lax.all_to_all(jnp.stack([nbr_embed] * lax.axis_size('nbr')), 'nbr', 0, 0)]
    unnamed x31 -> x33, local copies, waits for them, and re-layouts: 15.5 us -> 15.5 us
  transfers between devices with their start and end apart: 5 -> 5, of which waited for: 5 -> 4; matrix products, arithmetic and copies ran while one was open for 8% -> 8% of each run, Pallas kernels for 0% -> 0%
where the time goes in v1:
time: 386 us
  waiting for transfers between devices  283 us (73%)
  local copies, waits for them, and re-layouts  41.6 us (11%)
  matrix products  23.3 us (6%)
  between operations  14.1 us (4%)
  starting transfers between devices  12.4 us (3%)
  other arithmetic  11.5 us (3%)
    psum x1, waiting for transfers between devices, local(): lax.psum(jnp.dot(enc_att, enc_out, preferred_element_type=jnp.float32), '...  128 us
    all_to_all x1, waiting for transfers between devices, local(): lax.all_to_all(jnp.stack([nbr_embed] * lax.axis_size('nbr')), 'nbr', 0, 0)  92.9 us
    reduce_scatter x1, waiting for transfers between devices, local(): lax.psum_scatter(jnp.dot(cca_att, out_proj, preferred_element_type=jnp.fl...  58.2 us
    unnamed x33, local copies, waits for them, and re-layouts  15.5 us
    all_to_all x1, starting transfers between devices, local(): lax.all_to_all(jnp.stack([nbr_embed] * lax.axis_size('nbr')), 'nbr', 0, 0)  8.75 us
  transfers between devices with their start and end apart: 5, of which 4 were waited for; matrix products, arithmetic and copies ran while one was open for 8% of the time, Pallas kernels for 0%

profile of v1, /device:TPU:6, one launch (start us, length us, event | category | flops | bytes accessed | tf_op | source)
XLA Modules:
  0.0 385.6 jit_solution(11231546169543000472)
XLA Ops:
  7.2 3.4 stack.2
  10.6 8.7 %all-to-all-start = ((bf16[16,16,8,896]{3,2,1,0:T(8,128)(2,1)}), bf16[16,16,8,896]{3,2,1,0:T(8,128)(2,1)}, u32[]{:S(2)}, u32[]{:S(2)}) async-start(bf16[16,16,8,896]{3,2,1,0:T(8,128)(2,1)} %stack.2), calls=%async_computation | async-start | bytes 7340032 | tf_op jit(solution)/shard_map/all_to_all | solution.py:72
  19.4 0.7 all-gather.2.cloned.1.call-update
  20.4 8.7 %copy.46 = bf16[4096,3,256]{0,2,1:T(8,128)(2,1)} copy(bf16[4096,3,256]{2,0,1:T(8,128)(2,1)} %param.14) | data formatting | bytes 12582912 | tf_op args[4]
  29.2 92.9 %all-to-all-done = bf16[16,16,8,896]{3,2,1,0:T(8,128)(2,1)} async-done(((bf16[16,16,8,896]{3,2,1,0:T(8,128)(2,1)}), bf16[16,16,8,896]{3,2,1,0:T(8,128)(2,1)}, u32[]{:S(2)}, u32[]{:S(2)}) %all-to-all-start) | async-done | bytes 3670048 | tf_op jit(solution)/shard_map/all_to_all | solution.py:72
  122.1 4.4 %copy.72 = bf16[16,16,8,896]{3,2,0,1:T(8,128)(2,1)} copy(bf16[16,16,8,896]{3,2,1,0:T(8,128)(2,1)} %all-to-all-done) | data formatting | bytes 7340032 | tf_op jit(solution)/shard_map/all_to_all | solution.py:72
  126.4 4.8 %gather_fusion = bf16[16,128,896]{2,1,0:T(8,128)(2,1)} fusion(bf16[16,128,896]{2,1,0:T(8,128)(2,1)} %bitcast.54, s32[1024]{0:T(1024)S(1)} %pad_clamp_fusion), kind=kCustom, calls=%fused_computation | custom fusion | bytes 7340096 | tf_op jit(solution)/shard_map/jit(_take)/gather | solution.py:77
  131.2 2.4 bitcast_select_fusion
  133.7 2.3 convolution_convert_fusion.2
  135.9 1.3 reshape.174
  137.3 7.5 %convolution_convert_fusion.4 = bf16[512,768]{1,0:T(8,128)(2,1)S(1)} fusion(bf16[512,4096]{1,0:T(8,128)(2,1)} %all-gather.2.cloned.1.call-done, bf16[4096,768]{0,1:T(8,128)(2,1)} %bitcast.55), kind=kOutput, calls=%fused_computation.14 | convolution fusion | flops 3221618688 | bytes 11272192 | tf_op jit(solution)/shard_map/dot_general | solution.py:59
  144.8 0.9 fusion.25
  145.7 1.0 reshape.175
  147.2 1.0 copy-done.5
  148.4 1.0 reshape.173
  149.4 2.0 fusion.2
  152.5 4.3 %fusion.27 = f32[2048,896]{1,0:T(8,128)} fusion(bf16[2048,256]{0,1:T(8,128)(2,1)S(1)} %bitcast.56, bf16[256,896]{1,0:T(8,128)(2,1)S(1)} %copy-done.9), kind=kOutput, calls=%fused_computation.73 | convolution fusion | flops 939524096 | bytes 8847360 | tf_op jit(solution)/shard_map/dot_general | solution.py:92
  157.0 0.9 copy-done.7
  157.9 1.1 copy.56
  159.5 128.1 %all-reduce.2.cloned.1.call-done = f32[2048,896]{1,0:T(8,128)} async-done(((f32[2048,896]{1,0:T(8,128)}), f32[2048,896]{1,0:T(8,128)}) %all-reduce.2.cloned.1.call-update) | async-done | bytes 7340048 | tf_op jit(solution)/shard_map/psum | solution.py:92
  287.6 5.5 %multiply_reduce_fusion = f32[2048]{0:T(1024)S(1)} fusion(f32[2048,896]{1,0:T(8,128)} %all-reduce.2.cloned.1.call-done, bf16[16,128,896]{2,1,0:T(8,128)(2,1)} %gather_fusion, pred[2048]{0:T(1024)(128)(4,1)S(1)} %broadcast_bitcast_fusion), kind=kLoop, calls=%fused_computation.3 | loop fusion | flops 9172992 | bytes 11020288 | tf_op jit(solution)/shard_map/reduce_sum | solution.py:35
  293.1 1.9 copy-done.2
  295.0 1.9 multiply_convert_fusion
  297.0 2.4 convolution_convert_fusion.1
  299.4 1.3 copy-done.4
  300.7 3.4 collective-permute-start
  304.9 4.0 %concatenate.15 = bf16[8,256,2,2,128]{4,3,2,1,0:T(2,128)(2,1)} reshape(bf16[2048,512]{1,0:T(8,128)(2,1)} %copy-done.4) | data formatting | bytes 4194304 | tf_op jit(solution)/shard_map/concatenate | solution.py:102
  308.8 2.6 collective-permute-done
  311.6 2.3 copy_dynamic-update-slice_fusion
  315.9 3.3 convolution_convert_fusion
  319.2 1.6 constant_dynamic-slice_fusion
  320.8 58.2 %reduce-scatter.2.cloned.1.call-done = bf16[32,4096]{1,0:T(8,128)(2,1)} async-done(((bf16[512,4096]{1,0:T(8,128)(2,1)}), bf16[32,4096]{1,0:T(8,128)(2,1)}) %reduce-scatter.2.cloned.1.call-update) | async-done | bytes 262160 | tf_op jit(solution)/shard_map/reduce_scatter | solution.py:134
  (65 shorter events, 5.7 us)
Async XLA Ops:
  7.2 308.7 %copy-start = (bf16[256,4096]{1,0:T(8,128)(2,1)S(1)}, bf16[256,4096]{1,0:T(8,128)(2,1)}, u32[]{:S(2)}) copy-start(bf16[256,4096]{1,0:T(8,128)(2,1)} %param.19) | copy-start | bytes 6291460
  10.5 9.5 %copy-start.11 = (s32[8,2]{0,1:T(2,128)S(1)}, s32[8,2]{0,1:T(2,128)}, u32[]{:S(2)}) copy-start(s32[8,2]{0,1:T(2,128)} %param.12) | copy-start | bytes 196
  10.6 111.5 %all-to-all-start = ((bf16[16,16,8,896]{3,2,1,0:T(8,128)(2,1)}), bf16[16,16,8,896]{3,2,1,0:T(8,128)(2,1)}, u32[]{:S(2)}, u32[]{:S(2)}) async-start(bf16[16,16,8,896]{3,2,1,0:T(8,128)(2,1)} %stack.2), calls=%async_computation | async-start | bytes 7340032 | tf_op jit(solution)/shard_map/all_to_all | solution.py:72
  19.3 118.0 %all-gather.2.cloned.1.call-start = ((), (), s32[]{:S(2)}) async-start(), calls=%async_computation.2 | async-start | bytes 4456448 | tf_op jit(solution)/shard_map/all_gather | solution.py:60
  20.0 267.5 %all-reduce.2.cloned.1.call-start = ((), (), s32[]{:S(2)}) async-start(), calls=%async_computation.3 | async-start | bytes 14680064 | tf_op jit(solution)/shard_map/psum | solution.py:92
  131.2 2.4 copy-start.13
  147.2 1.0 copy-start.5
  151.5 1.0 copy-start.9
  156.8 1.2 copy-start.7
  156.8 2.3 copy-start.12
  156.8 222.3 %reduce-scatter.2.cloned.1.call-start = ((), (), s32[]{:S(2)}) async-start(), calls=%async_computation.4 | async-start | bytes 4456448 | tf_op jit(solution)/shard_map/reduce_scatter | solution.py:134
  159.5 133.6 %copy-start.10 = (f32[896]{0:T(1024)S(1)}, f32[896]{0:T(1024)}, u32[]{:S(2)}) copy-start(f32[896]{0:T(1024)} %param.17) | copy-start | bytes 10756
  287.6 5.5 %copy-start.1 = (bf16[16,128,896]{2,1,0:T(8,128)(2,1)S(1)}, bf16[16,128,896]{2,1,0:T(8,128)(2,1)}, u32[]{:S(2)}) copy-start(bf16[16,128,896]{2,1,0:T(8,128)(2,1)} %gather_fusion) | copy-start | bytes 11010052
  287.6 7.4 %copy-start.2 = (f32[2048,896]{1,0:T(8,128)S(1)}, f32[2048,896]{1,0:T(8,128)}, u32[]{:S(2)}) copy-start(f32[2048,896]{1,0:T(8,128)} %all-reduce.2.cloned.1.call-done) | copy-start | bytes 22020100
  295.0 1.9 copy-start.8
  296.9 2.4 copy-start.3
  297.0 7.6 %copy-start.6 = (bf16[512,256]{1,0:T(8,128)(2,1)S(1)}, bf16[512,256]{1,0:T(8,128)(2,1)}, u32[]{:S(2)}) copy-start(bf16[512,256]{1,0:T(8,128)(2,1)} %get-tuple-element.2) | copy-start | bytes 786436
  299.3 1.3 copy-start.4
  300.7 10.8 %collective-permute-start = (bf16[256,512]{1,0:T(8,128)(2,1)S(1)}, bf16[256,512]{1,0:T(8,128)(2,1)S(1)}, u32[]{:S(2)}, u32[]{:S(2)}) collective-permute-start(bf16[256,512]{1,0:T(8,128)(2,1)S(1)} %slice.34), channel_id=1, source_target_pairs={{0,16},{16,32},{32,48},{48,64},{64,80},{80,96},{96,112},{112,128},... | collective-permute-start | bytes 786440 | tf_op jit(solution)/shard_map/ppermute | solution.py:15
Sparse Core Ops, SparseCore 0:
  22.0 99.0 all-gather.1
  156.9 130.6 all-reduce.1
  319.3 59.7 reduce-scatter.1
